TPU v7x, 512 devices: a whole 4x8x8 slice. The times are simulated.
512 devices in a mesh: dp: 16 (over z, core), tensor: 32 (over x, y).
Axes of the slice: x: 4, y: 8, z: 8, core: 2. Of those that a mesh axis runs over, the one named last changes fastest.
Arguments:
- activations: bfloat16 [12288, 4096], P('dp', 'tensor'), may hold values from -6 to 6
- out_grads_t: bfloat16 [5504, 12288], P('tensor', 'dp'), may hold values from -6 to 6
- in_basis: bfloat16 [4096, 4096], P(None, 'tensor'), may hold values from -0.09375 to 0.09375
- out_basis_t: bfloat16 [5504, 5504], P('tensor'), may hold values from -0.078125 to 0.078125
- query_proj: bfloat16 [4, 5504, 4096], P(None, 'tensor', 'dp'), may hold values from -6 to 6
- eigvals: float32 [5504, 4096], P('tensor', 'dp'), may hold values from 0.05 to 5
- damping: float32 [1], replicated, may hold values from 0.05 to 0.2
- lengths: int32 [96], P('dp'), may hold values from 1 to 128, 7680 in all
Outputs:
- scores: float32 [96, 4], P('dp')
Inputs may be any that keep to these rules, and one draw needn't show every extreme that they name: `lengths`: the largest token count is exactly 128.
All inputs are finite; a program needn't handle non-finite values. No bound on the sum of `lengths` on one device may be relied on, other than what follows from the above.
Results may differ from a plain program's by a relative error of at most 0.006.
Values may be sent and summed in bfloat16 or wider, within the bound.
No kernel may reach another device: no remote copies, remote signals or barrier semaphores. Data moves between devices by JAX's collectives and lax.ppermute only.
A program may use at most 128 MiB of HBM per device.

v0:
```python
import jax
import jax.numpy as jnp
from jax import lax
from jax.sharding import PartitionSpec as P


def local(activations, out_grads_t, in_basis, out_basis_t, query_proj, eigvals, damping, lengths):
    full_act = lax.all_gather(activations, "tensor", axis=1, tiled=True)
    act_local = jnp.dot(full_act, in_basis, preferred_element_type=jnp.float32).astype(jnp.bfloat16)
    act_proj = lax.all_gather(act_local, "tensor", axis=1, tiled=True)
    token_rows = full_act.shape[0]
    width = out_basis_t.shape[0]
    grad_full = jnp.dot(
        out_basis_t,
        lax.all_gather(out_grads_t, "tensor", axis=0, tiled=True),
        preferred_element_type=jnp.float32,
    )
    seq_count = lengths.shape[0]
    seq_len = token_rows // seq_count
    position = lax.broadcasted_iota(jnp.int32, (seq_count, seq_len), 1)
    keep = (position < lengths[:, None]).astype(jnp.float32).reshape(1, token_rows)
    grad_proj = (grad_full * keep).astype(jnp.bfloat16)
    scaled = (query_proj.astype(jnp.float32) / (eigvals + damping[0])).astype(jnp.bfloat16)
    projected = jnp.einsum(
        "jst,std->sjd",
        grad_proj.reshape(width, seq_count, seq_len),
        act_proj.reshape(seq_count, seq_len, act_proj.shape[1]),
        preferred_element_type=jnp.float32,
    )
    partial_value = jnp.einsum(
        "sij,qij->sq",
        projected,
        lax.all_gather(scaled, "dp", axis=2, tiled=True).astype(jnp.float32),
    )
    totals = lax.psum(partial_value, "tensor")
    norm_factor = (act_proj.shape[1] * out_basis_t.shape[1] * seq_len) ** (-0.5)
    return totals * norm_factor


def solution(mesh):
    placed = (
        P("dp", "tensor"),
        P("tensor", "dp"),
        P(None, "tensor"),
        P("tensor", None),
        P(None, "tensor", "dp"),
        P("tensor", "dp"),
        P(),
        P("dp"),
    )
    return jax.shard_map(
        local, mesh=mesh, in_specs=placed, out_specs=P("dp", None), check_vma=False
    )
```

profile of v0, /device:TPU:64, one launch (start us, length us, event | category | flops | bytes accessed | tf_op | source)
XLA Modules:
  0.0 474.7 jit_solution(10755105774203012612)
XLA Ops:
  6.5 0.0 copy-start
  6.5 0.0 all-gather.6.cloned.1.call-start
  6.6 0.7 all-gather.6.cloned.1.call-update
  7.3 0.0 all-gather.12.cloned.1.call-start
  7.3 0.7 all-gather.12.cloned.1.call-update
  8.0 0.0 all-gather.8.cloned.1.call-start
  8.1 104.2 %all-gather.6.cloned.1.call-done = bf16[768,4096]{1,0:T(8,128)(2,1)} async-done(((bf16[768,128]{1,0:T(8,128)(2,1)}), bf16[768,4096]{1,0:T(8,128)(2,1)}) %all-gather.6.cloned.1.call-update) | async-done | bytes 6291472 | tf_op jit(solution)/shard_map/all_gather | solution.py:8
  112.3 5.5 %convolution_convert_fusion = bf16[768,128]{1,0:T(8,128)(2,1)} fusion(bf16[768,4096]{1,0:T(8,128)(2,1)} %all-gather.6.cloned.1.call-done, bf16[4096,128]{1,0:T(8,128)(2,1)} %param.10), kind=kOutput, calls=%fused_computation.4 | convolution fusion | flops 805404672 | bytes 7536640 | tf_op jit(solution)/shard_map/dot_general | solution.py:9
  117.8 0.0 all-gather.8.cloned.1.call-update
  117.8 0.0 all-gather.10.cloned.1.call-start
  118.5 0.0 copy-done.2
  118.5 0.9 fusion.6
  119.5 0.0 all-gather.10.cloned.1.call-update
  119.5 0.1 convert_bitcast_fusion
  119.6 100.5 %all-gather.12.cloned.1.call-done = bf16[32,172,768]{2,1,0:T(8,128)(2,1)} async-done(((bf16[1,172,768]{2,1,0:T(8,128)(2,1)}), bf16[32,172,768]{2,1,0:T(8,128)(2,1)}) %all-gather.12.cloned.1.call-update) | async-done | bytes 8454160 | tf_op jit(solution)/shard_map/all_gather | solution.py:15
  220.1 12.5 %reshape.30 = bf16[5504,768]{1,0:T(8,128)(2,1)} reshape(bf16[32,172,768]{2,1,0:T(8,128)(2,1)} %all-gather.12.cloned.1.call-done) | data formatting | bytes 16908288
  232.6 5.2 %fusion.2 = bf16[172,768]{1,0:T(8,128)(2,1)S(1)} fusion(bf16[172,5504]{1,0:T(8,128)(2,1)S(1)} %copy-done, bf16[5504,768]{1,0:T(8,128)(2,1)} %reshape.30, f32[768]{0:T(1024)S(1)} %convert_bitcast_fusion), kind=kOutput, calls=%fused_computation.3 | convolution fusion | flops 1454376960 | bytes 10614784 | tf_op jit(solution)/shard_map/dot_general | solution.py:13
  237.7 0.3 reshape.26
  238.0 80.5 %all-gather.8.cloned.1.call-done = bf16[768,4096]{1,0:T(8,128)(2,1)} async-done(((bf16[768,128]{1,0:T(8,128)(2,1)}), bf16[768,4096]{1,0:T(8,128)(2,1)}) %all-gather.8.cloned.1.call-update) | async-done | bytes 6291472 | tf_op jit(solution)/shard_map/all_gather | solution.py:10
  318.6 8.5 %fusion.7 = bf16[6,172,4096]{2,1,0:T(8,128)(2,1)} fusion(bf16[6,128,4096]{2,1,0:T(8,128)(2,1)} %bitcast.14, bf16[172,6,128]{2,1,0:T(8,128)(2,1)S(1)} %reshape.26), kind=kOutput, calls=%fused_computation.8 | convolution fusion | flops 1082130432 | bytes 15009792 | tf_op jit(solution)/shard_map/jst,std->sjd/dot_general | solution.py:24
  327.1 51.2 %all-gather.10.cloned.1.call-done = bf16[4,172,4096]{2,0,1:T(4,128)(2,1)} async-done(((bf16[4,172,256]{2,0,1:T(4,128)(2,1)}), bf16[4,172,4096]{2,0,1:T(4,128)(2,1)}) %all-gather.10.cloned.1.call-update) | async-done | bytes 5636112 | tf_op jit(solution)/shard_map/all_gather | solution.py:33
  378.3 15.5 %fusion.3 = f32[6,4]{0,1:T(4,128)S(1)} fusion(bf16[4,172,4096]{2,0,1:T(4,128)(2,1)} %all-gather.10.cloned.1.call-done, bf16[6,172,4096]{2,1,0:T(8,128)(2,1)} %fusion.7), kind=kOutput, calls=%fused_computation.5 | convolution fusion | flops 33816576 | bytes 14090336 | tf_op jit(solution)/shard_map/sij,qij->sq/dot_general | solution.py:30
  393.8 73.8 %psum.7 = f32[6,4]{0,1:T(4,128)S(1)} all-reduce(f32[6,4]{0,1:T(4,128)S(1)} %fusion.3), channel_id=1, replica_groups=mesh['dp'=16,'tensor'=32] {'tensor'}, use_global_device_ids=true, to_apply=%region_0.0 | all-reduce | flops 24 | bytes 192 | tf_op jit(solution)/shard_map/psum | solution.py:35
  467.6 0.6 broadcast_multiply_fusion
  (7 shorter events, 0.0 us)
Async XLA Ops:
  6.5 226.0 %copy-start = (bf16[172,5504]{1,0:T(8,128)(2,1)S(1)}, bf16[172,5504]{1,0:T(8,128)(2,1)}, u32[]{:S(2)}) copy-start(bf16[172,5504]{1,0:T(8,128)(2,1)} %param.11) | copy-start | bytes 5680132
  6.5 111.9 %copy-start.2 = (f32[172,256]{1,0:T(8,128)S(1)}, f32[172,256]{1,0:T(8,128)}, u32[]{:S(2)}) copy-start(f32[172,256]{1,0:T(8,128)} %param.13) | copy-start | bytes 528388
  6.5 112.0 %copy-start.1 = (bf16[4,172,256]{2,0,1:T(4,128)(2,1)S(1)}, bf16[4,172,256]{2,0,1:T(4,128)(2,1)}, u32[]{:S(2)}) copy-start(bf16[4,172,256]{2,0,1:T(4,128)(2,1)} %param.12) | copy-start | bytes 1056772
  6.5 112.9 %copy-start.3 = (s32[6]{0:T(128)S(1)}, s32[6]{0:T(128)}, u32[]{:S(2)}) copy-start(s32[6]{0:T(128)} %param.15) | copy-start | bytes 76
  6.5 105.7 %all-gather.6.cloned.1.call-start = ((), (), s32[]{:S(2)}) async-start(), calls=%async_computation | async-start | bytes 6488064 | tf_op jit(solution)/shard_map/all_gather | solution.py:8
  7.3 212.8 %all-gather.12.cloned.1.call-start = ((), (), s32[]{:S(2)}) async-start(), calls=%async_computation.3 | async-start | bytes 8921088 | tf_op jit(solution)/shard_map/all_gather | solution.py:15
  8.0 310.6 %all-gather.8.cloned.1.call-start = ((), (), s32[]{:S(2)}) async-start(), calls=%async_computation.1 | async-start | bytes 6488064 | tf_op jit(solution)/shard_map/all_gather | solution.py:10
  117.8 260.5 %all-gather.10.cloned.1.call-start = ((), (), s32[]{:S(2)}) async-start(), calls=%async_computation.2 | async-start | bytes 5988352 | tf_op jit(solution)/shard_map/all_gather | solution.py:33
Sparse Core Ops, SparseCore 0:
  10.4 101.8 all-gather.5
  115.4 104.6 all-gather.11
  223.1 95.4 all-gather.7
  320.5 57.7 all-gather.9
where the time goes:
time: 475 us
  waiting for transfers between devices  338 us (71%)
  blocking collectives  73.8 us (16%)
  matrix products  34.7 us (7%)
  between operations  13.8 us (3%)
  local copies, waits for them, and re-layouts  12.8 us (3%)
    all_gather x1, waiting for transfers between devices, local(): full_act = lax.all_gather(activations, 'tensor', axis=1, tiled=True)  104 us
    all_gather x1, waiting for transfers between devices, local(): lax.all_gather(out_grads_t, 'tensor', axis=0, tiled=True)  101 us
    all_gather x1, waiting for transfers between devices, local(): act_proj = lax.all_gather(act_local, 'tensor', axis=1, tiled=True)  80.5 us
    psum x1, blocking collectives, local(): totals = lax.psum(partial_value, 'tensor')  73.8 us
    all_gather x1, waiting for transfers between devices, local(): lax.all_gather(scaled, 'dp', axis=2, tiled=True).astype(jnp.float32)  51.2 us
    dot_general x1, matrix products, local(): jnp.einsum('sij,qij->sq', projected, lax.all_gather(scaled, 'dp', axis=2,...  15.5 us
    unnamed x9, local copies, waits for them, and re-layouts  12.5 us
  transfers between devices with their start and end apart: 4, of which 4 were waited for; matrix products, arithmetic and copies ran while one was open for 7% of the time, Pallas kernels for 0%

commit v1 on v0

--- a/solution.py
+++ b/solution.py
@@ -32,7 +32,9 @@
         projected,
         lax.all_gather(scaled, "dp", axis=2, tiled=True).astype(jnp.float32),
     )
-    totals = lax.psum(partial_value, "tensor")
+    totals = partial_value
+    for hop in (1, 2, 4, 8, 16):
+        totals = totals + lax.ppermute(totals, "tensor", [(dev, dev ^ hop) for dev in range(32)])
     norm_factor = (act_proj.shape[1] * out_basis_t.shape[1] * seq_len) ** (-0.5)
     return totals * norm_factor
 

time: 475 us -> 435 us (0.916)
  blocking collectives: 73.8 us -> 0 us
  starting transfers between devices: 0.15 us -> 19.6 us
  waiting for transfers between devices: 338 us -> 352 us
    psum x1 -> x0, blocking collectives: 73.8 us -> none  [local(): totals = lax.psum(partial_value, 'tensor')]
    ppermute x0 -> x5, starting transfers between devices: none -> 19.4 us  [local(): lax.ppermute(totals, 'tensor', [(dev, dev ^ hop) for dev in range(32)])]
    ppermute x0 -> x5, waiting for transfers between devices: none -> 14.2 us  [local(): lax.ppermute(totals, 'tensor', [(dev, dev ^ hop) for dev in range(32)])]
  transfers between devices with their start and end apart: 4 -> 9, of which waited for: 4 -> 9; matrix products, arithmetic and copies ran while one was open for 7% -> 8% of each run, Pallas kernels for 0% -> 0%
where the time goes in v1:
time: 435 us
  waiting for transfers between devices  352 us (81%)
  matrix products  34.7 us (8%)
  starting transfers between devices  19.6 us (5%)
  between operations  13.9 us (3%)
  local copies, waits for them, and re-layouts  12.8 us (3%)
    all_gather x1, waiting for transfers between devices, local(): full_act = lax.all_gather(activations, 'tensor', axis=1, tiled=True)  104 us
    all_gather x1, waiting for transfers between devices, local(): lax.all_gather(out_grads_t, 'tensor', axis=0, tiled=True)  100 us
    all_gather x1, waiting for transfers between devices, local(): act_proj = lax.all_gather(act_local, 'tensor', axis=1, tiled=True)  80.5 us
    all_gather x1, waiting for transfers between devices, local(): lax.all_gather(scaled, 'dp', axis=2, tiled=True).astype(jnp.float32)  51.2 us
    ppermute x5, starting transfers between devices, local(): lax.ppermute(totals, 'tensor', [(dev, dev ^ hop) for dev in range(32)])  19.4 us
    dot_general x1, matrix products, local(): jnp.einsum('sij,qij->sq', projected, lax.all_gather(scaled, 'dp', axis=2,...  15.5 us
    ppermute x5, waiting for transfers between devices, local(): lax.ppermute(totals, 'tensor', [(dev, dev ^ hop) for dev in range(32)])  14.2 us
    unnamed x9, local copies, waits for them, and re-layouts  12.5 us
  transfers between devices with their start and end apart: 9, of which 9 were waited for; matrix products, arithmetic and copies ran while one was open for 8% of the time, Pallas kernels for 0%

profile of v1, /device:TPU:64, one launch (start us, length us, event | category | flops | bytes accessed | tf_op | source)
XLA Modules:
  0.0 434.6 jit_solution(17590614171788679808)
XLA Ops:
  6.6 0.7 all-gather.6.cloned.1.call-update
  7.3 0.7 all-gather.12.cloned.1.call-update
  8.1 104.2 %all-gather.6.cloned.1.call-done = bf16[768,4096]{1,0:T(8,128)(2,1)} async-done(((bf16[768,128]{1,0:T(8,128)(2,1)}), bf16[768,4096]{1,0:T(8,128)(2,1)}) %all-gather.6.cloned.1.call-update) | async-done | bytes 6291472 | tf_op jit(solution)/shard_map/all_gather | solution.py:8
  112.3 5.5 %convolution_convert_fusion = bf16[768,128]{1,0:T(8,128)(2,1)} fusion(bf16[768,4096]{1,0:T(8,128)(2,1)} %all-gather.6.cloned.1.call-done, bf16[4096,128]{1,0:T(8,128)(2,1)} %param.10), kind=kOutput, calls=%fused_computation.4 | convolution fusion | flops 805404672 | bytes 7536640 | tf_op jit(solution)/shard_map/dot_general | solution.py:9
  118.5 1.0 fusion.6
  119.6 100.5 %all-gather.12.cloned.1.call-done = bf16[32,172,768]{2,1,0:T(8,128)(2,1)} async-done(((bf16[1,172,768]{2,1,0:T(8,128)(2,1)}), bf16[32,172,768]{2,1,0:T(8,128)(2,1)}) %all-gather.12.cloned.1.call-update) | async-done | bytes 8454160 | tf_op jit(solution)/shard_map/all_gather | solution.py:15
  220.1 12.5 %reshape.30 = bf16[5504,768]{1,0:T(8,128)(2,1)} reshape(bf16[32,172,768]{2,1,0:T(8,128)(2,1)} %all-gather.12.cloned.1.call-done) | data formatting | bytes 16908288
  232.6 5.2 %fusion.2 = bf16[172,768]{1,0:T(8,128)(2,1)S(1)} fusion(bf16[172,5504]{1,0:T(8,128)(2,1)S(1)} %copy-done, bf16[5504,768]{1,0:T(8,128)(2,1)} %reshape.30, f32[768]{0:T(1024)S(1)} %convert_bitcast_fusion), kind=kOutput, calls=%fused_computation.3 | convolution fusion | flops 1454376960 | bytes 10614784 | tf_op jit(solution)/shard_map/dot_general | solution.py:13
  237.7 0.3 reshape.26
  238.1 80.5 %all-gather.8.cloned.1.call-done = bf16[768,4096]{1,0:T(8,128)(2,1)} async-done(((bf16[768,128]{1,0:T(8,128)(2,1)}), bf16[768,4096]{1,0:T(8,128)(2,1)}) %all-gather.8.cloned.1.call-update) | async-done | bytes 6291472 | tf_op jit(solution)/shard_map/all_gather | solution.py:10
  318.6 8.5 %fusion.7 = bf16[6,172,4096]{2,1,0:T(8,128)(2,1)} fusion(bf16[6,128,4096]{2,1,0:T(8,128)(2,1)} %bitcast.14, bf16[172,6,128]{2,1,0:T(8,128)(2,1)S(1)} %reshape.26), kind=kOutput, calls=%fused_computation.8 | convolution fusion | flops 1082130432 | bytes 15009792 | tf_op jit(solution)/shard_map/jst,std->sjd/dot_general | solution.py:24
  327.1 51.2 %all-gather.10.cloned.1.call-done = bf16[4,172,4096]{2,0,1:T(4,128)(2,1)} async-done(((bf16[4,172,256]{2,0,1:T(4,128)(2,1)}), bf16[4,172,4096]{2,0,1:T(4,128)(2,1)}) %all-gather.10.cloned.1.call-update) | async-done | bytes 5636112 | tf_op jit(solution)/shard_map/all_gather | solution.py:33
  378.3 15.5 %fusion.3 = f32[6,4]{0,1:T(4,128)S(1)} fusion(bf16[4,172,4096]{2,0,1:T(4,128)(2,1)} %all-gather.10.cloned.1.call-done, bf16[6,172,4096]{2,1,0:T(8,128)(2,1)} %fusion.7), kind=kOutput, calls=%fused_computation.5 | convolution fusion | flops 33816576 | bytes 14090336 | tf_op jit(solution)/shard_map/sij,qij->sq/dot_general | solution.py:30
  393.8 2.6 collective-permute-start
  396.4 2.8 collective-permute-done
  399.3 3.5 collective-permute-start.1
  402.8 2.8 collective-permute-done.1
  405.7 6.6 %collective-permute-start.2 = (f32[6,4]{0,1:T(4,128)S(1)}, f32[6,4]{0,1:T(4,128)S(1)}, u32[]{:S(2)}, u32[]{:S(2)}) collective-permute-start(f32[6,4]{0,1:T(4,128)S(1)} %add.24), channel_id=1, source_target_pairs={{0,4},{1,5},{2,6},{3,7},{4,0},{5,1},{6,2},{7,3},{8,12},{9,13},{10,... | collective-permute-start | bytes 296 | tf_op jit(solution)/shard_map/ppermute | solution.py:37
  412.3 2.8 collective-permute-done.2
  415.0 2.6 collective-permute-start.3
  417.6 2.9 collective-permute-done.3
  420.5 4.1 collective-permute-start.4
  424.6 2.9 collective-permute-done.4
  427.5 0.6 add_multiply_fusion
  (20 shorter events, 0.3 us)
Async XLA Ops:
  6.5 226.0 %copy-start = (bf16[172,5504]{1,0:T(8,128)(2,1)S(1)}, bf16[172,5504]{1,0:T(8,128)(2,1)}, u32[]{:S(2)}) copy-start(bf16[172,5504]{1,0:T(8,128)(2,1)} %param.11) | copy-start | bytes 5680132
  6.5 112.0 %copy-start.2 = (f32[172,256]{1,0:T(8,128)S(1)}, f32[172,256]{1,0:T(8,128)}, u32[]{:S(2)}) copy-start(f32[172,256]{1,0:T(8,128)} %param.13) | copy-start | bytes 528388
  6.5 112.0 %copy-start.1 = (bf16[4,172,256]{2,0,1:T(4,128)(2,1)S(1)}, bf16[4,172,256]{2,0,1:T(4,128)(2,1)}, u32[]{:S(2)}) copy-start(bf16[4,172,256]{2,0,1:T(4,128)(2,1)} %param.12) | copy-start | bytes 1056772
  6.5 113.0 %copy-start.3 = (s32[6]{0:T(128)S(1)}, s32[6]{0:T(128)}, u32[]{:S(2)}) copy-start(s32[6]{0:T(128)} %param.15) | copy-start | bytes 76
  6.5 105.7 %all-gather.6.cloned.1.call-start = ((), (), s32[]{:S(2)}) async-start(), calls=%async_computation | async-start | bytes 6488064 | tf_op jit(solution)/shard_map/all_gather | solution.py:8
  7.3 212.8 %all-gather.12.cloned.1.call-start = ((), (), s32[]{:S(2)}) async-start(), calls=%async_computation.3 | async-start | bytes 8921088 | tf_op jit(solution)/shard_map/all_gather | solution.py:15
  8.0 310.6 %all-gather.8.cloned.1.call-start = ((), (), s32[]{:S(2)}) async-start(), calls=%async_computation.1 | async-start | bytes 6488064 | tf_op jit(solution)/shard_map/all_gather | solution.py:10
  117.8 260.5 %all-gather.10.cloned.1.call-start = ((), (), s32[]{:S(2)}) async-start(), calls=%async_computation.2 | async-start | bytes 5988352 | tf_op jit(solution)/shard_map/all_gather | solution.py:33
  393.8 5.5 %collective-permute-start = (f32[6,4]{0,1:T(4,128)S(1)}, f32[6,4]{0,1:T(4,128)S(1)}, u32[]{:S(2)}, u32[]{:S(2)}) collective-permute-start(f32[6,4]{0,1:T(4,128)S(1)} %fusion.3), channel_id=1, source_target_pairs={{0,1},{1,0},{2,3},{3,2},{4,5},{5,4},{6,7},{7,6},{8,9},{9,8},{10,11... | collective-permute-start | bytes 296 | tf_op jit(solution)/shard_map/ppermute | solution.py:37
  399.3 6.4 %collective-permute-start.1 = (f32[6,4]{0,1:T(4,128)S(1)}, f32[6,4]{0,1:T(4,128)S(1)}, u32[]{:S(2)}, u32[]{:S(2)}) collective-permute-start(f32[6,4]{0,1:T(4,128)S(1)} %add.23), channel_id=1, source_target_pairs={{0,2},{1,3},{2,0},{3,1},{4,6},{5,7},{6,4},{7,5},{8,10},{9,11},{10,... | collective-permute-start | bytes 296 | tf_op jit(solution)/shard_map/ppermute | solution.py:37
  405.7 9.4 %collective-permute-start.2 = (f32[6,4]{0,1:T(4,128)S(1)}, f32[6,4]{0,1:T(4,128)S(1)}, u32[]{:S(2)}, u32[]{:S(2)}) collective-permute-start(f32[6,4]{0,1:T(4,128)S(1)} %add.24), channel_id=1, source_target_pairs={{0,4},{1,5},{2,6},{3,7},{4,0},{5,1},{6,2},{7,3},{8,12},{9,13},{10,... | collective-permute-start | bytes 296 | tf_op jit(solution)/shard_map/ppermute | solution.py:37
  415.0 5.5 %collective-permute-start.3 = (f32[6,4]{0,1:T(4,128)S(1)}, f32[6,4]{0,1:T(4,128)S(1)}, u32[]{:S(2)}, u32[]{:S(2)}) collective-permute-start(f32[6,4]{0,1:T(4,128)S(1)} %add.25), channel_id=1, source_target_pairs={{0,8},{1,9},{2,10},{3,11},{4,12},{5,13},{6,14},{7,15},{8,0},{9,1},... | collective-permute-start | bytes 296 | tf_op jit(solution)/shard_map/ppermute | solution.py:37
  420.5 7.0 %collective-permute-start.4 = (f32[6,4]{0,1:T(4,128)S(1)}, f32[6,4]{0,1:T(4,128)S(1)}, u32[]{:S(2)}, u32[]{:S(2)}) collective-permute-start(f32[6,4]{0,1:T(4,128)S(1)} %add.26), channel_id=1, source_target_pairs={{0,16},{1,17},{2,18},{3,19},{4,20},{5,21},{6,22},{7,23},{8,24},{9,... | collective-permute-start | bytes 296 | tf_op jit(solution)/shard_map/ppermute | solution.py:37
Sparse Core Ops, SparseCore 0:
  10.4 101.8 all-gather.5
  115.4 104.6 all-gather.11
  223.1 95.4 all-gather.7
  320.5 57.7 all-gather.9
